TPU v7x, 256 devices: a whole 4x4x8 slice. The times are simulated.
256 devices in a mesh: group: 64 (over y, z, core), rep: 4 (over x).
Axes of the slice: x: 4, y: 4, z: 8, core: 2. Of those that a mesh axis runs over, the one named last changes fastest.
Arguments:
- tokens: bfloat16 [8192, 4096], P('group', 'rep'), may hold values from -6 to 6
- affinity: float32 [8192, 64], P(('group', 'rep')), may hold values from -4.5 to 4.5
- gumbel_perturbation: float32 [8192, 64], P(('group', 'rep')), may hold values from -2 to 7
- expert_assignment: int32 [8192, 1], P('group'), may hold values from 0 to 63; in each aligned block of 128 rows (0 to 127, 128 to 255, ...) at most 4 rows name the same one
- expert_gate: bfloat16 [64, 4096, 2048], P('group', None, 'rep'), may hold values from -0.09375 to 0.09375
- expert_up: bfloat16 [64, 4096, 2048], P('group', None, 'rep'), may hold values from -0.09375 to 0.09375
- expert_down: bfloat16 [64, 2048, 4096], P('group', 'rep'), may hold values from -0.125 to 0.125
Outputs:
- combined: bfloat16 [8192, 4096], P('group', 'rep')
Inputs may be any that keep to these rules, and one draw needn't show every extreme that they name: `expert_assignment`: among the tokens of one index of group (aligned blocks of 128 rows), at most 4 name the same expert.
All inputs are finite; a program needn't handle non-finite values.
Results may differ from a plain program's by a relative error of at most 0.0057.
Values may be sent and summed in bfloat16 or wider, within the bound.
A program may use at most 320 MiB of HBM per device.

v0:
```python
import jax
import jax.numpy as jnp
from jax import lax
from jax.sharding import PartitionSpec as P

PASSES = 3


def local(
    tokens, affinity, gumbel_perturbation, expert_assignment, expert_gate, expert_up, expert_down
):
    tok_count = tokens.shape[0]
    quarter = tokens.shape[1]
    experts = affinity.shape[1]
    own_rows = affinity.shape[0]
    expert_groupings = lax.axis_size("group")
    total = tok_count * expert_groupings
    capacity = max(2, 2 * tok_count // expert_groupings)
    flattened_expert_index = expert_assignment[:, 0]
    kernel = jnp.exp(affinity + gumbel_perturbation)
    row_scale = jnp.ones((own_rows,), jnp.float32)
    col_scale = jnp.ones((experts,), jnp.float32)
    for number in range(PASSES):
        column = lax.psum(jnp.sum(kernel * row_scale[:, None], axis=0), ("group", "rep"))
        col_scale = total / experts / column
        row_scale = 1.0 / jnp.sum(kernel * col_scale[None, :], axis=1)
    offset = lax.axis_index("rep") * own_rows
    own_ids = lax.dynamic_slice_in_dim(flattened_expert_index, offset, own_rows, 0)
    picked = jax.nn.one_hot(own_ids, experts, dtype=jnp.float32)
    own_weights = experts * row_scale * jnp.sum(picked * kernel * col_scale[None, :], axis=1)
    routing_weight = lax.all_gather(own_weights, "rep", axis=0, tiled=True)
    chosen_int = jax.nn.one_hot(flattened_expert_index, experts, dtype=jnp.int32)
    earlier = jnp.cumsum(chosen_int, axis=0) - 1
    slot_index = jnp.sum(chosen_int * earlier, axis=1)
    target = flattened_expert_index * capacity + slot_index
    placer = (jnp.arange(experts * capacity, dtype=jnp.int32)[:, None] == target[None, :]).astype(
        jnp.bfloat16
    )
    outgoing = jnp.dot(placer, tokens, preferred_element_type=jnp.float32).astype(jnp.bfloat16)
    outgoing = outgoing.reshape(experts, capacity, quarter)
    full_rows = lax.all_gather(
        lax.all_to_all(outgoing, "group", split_axis=0, concat_axis=0, tiled=True),
        "rep",
        axis=2,
        tiled=True,
    )
    width = full_rows.shape[2]
    flattened = full_rows.reshape(-1, width)
    gate_term = jnp.dot(flattened, expert_gate[0], preferred_element_type=jnp.float32)
    up_projection_term = jnp.dot(flattened, expert_up[0], preferred_element_type=jnp.float32)
    hidden = (jax.nn.silu(gate_term) * up_projection_term).astype(jnp.bfloat16)
    partial_output_rows = jnp.dot(
        hidden, expert_down[0], preferred_element_type=jnp.float32
    ).reshape(full_rows.shape)
    summed = lax.psum_scatter(partial_output_rows, "rep", scatter_dimension=2, tiled=True).astype(
        jnp.bfloat16
    )
    returned = lax.all_to_all(summed, "group", split_axis=0, concat_axis=0, tiled=True)
    flat_back = returned.reshape(experts * capacity, quarter)
    home_rows = lax.dot_general(
        placer, flat_back, (((0,), (0,)), ((), ())), preferred_element_type=jnp.float32
    )
    return (routing_weight[:, None] * home_rows).astype(jnp.bfloat16)


def solution(mesh):
    return jax.shard_map(
        local,
        mesh=mesh,
        in_specs=(
            P("group", "rep"),
            P(("group", "rep"), None),
            P(("group", "rep"), None),
            P("group", None),
            P("group", None, "rep"),
            P("group", None, "rep"),
            P("group", "rep", None),
        ),
        out_specs=P("group", "rep"),
        check_vma=False,
    )
```

profile of v0, /device:TPU:1, one launch (start us, length us, event | category | flops | bytes accessed | tf_op | source)
XLA Modules:
  0.0 339.7 jit_solution(9259441102689474174)
XLA Ops:
  6.5 0.0 copy-start
  6.5 0.0 all-gather.2.cloned.1.call-start
  6.5 0.8 fusion.16
  7.3 0.2 reduce_window_sum.11
  7.5 0.8 select_reduce_fusion
  8.3 0.7 multiply_add_fusion
  9.0 0.0 copy-done
  9.0 0.3 convolution_convert_fusion
  9.3 0.2 reshape.31
  9.5 30.4 %all_to_all.10 = bf16[64,4,1024]{2,1,0:T(4,128)(2,1)} all-to-all(bf16[64,4,1024]{2,1,0:T(4,128)(2,1)S(1)} %reshape.31), channel_id=1, replica_groups=mesh['group'=64,'rep'=4] {'group'}, dimensions={0} | all-to-all | bytes 1048576 | tf_op jit(solution)/shard_map/all_to_all | solution.py:42
  39.9 0.0 all-gather.2.cloned.1.call-update
  39.9 0.0 reduce-scatter.2.cloned.1.call-start
  40.0 30.4 %all-gather.2.cloned.1.call-done = bf16[64,4,4096]{2,1,0:T(4,128)(2,1)} async-done(((bf16[64,4,1024]{2,1,0:T(4,128)(2,1)}), bf16[64,4,4096]{2,1,0:T(4,128)(2,1)}) %all-gather.2.cloned.1.call-update) | async-done | bytes 2097168 | tf_op jit(solution)/shard_map/all_gather | solution.py:41
  70.3 2.5 reshape.32
  72.9 0.0 copy-start.4
  72.9 3.6 %fusion.4 = f32[256,512]{1,0:T(8,128)S(1)} fusion(bf16[256,4096]{1,0:T(8,128)(2,1)S(1)} %reshape.32, bf16[1,4096,512]{2,1,0:T(8,128)(2,1)} %param.11), kind=kOutput, calls=%fused_computation.4 | convolution fusion | flops 1073741824 | bytes 6815744 | tf_op jit(solution)/shard_map/dot_general | solution.py:49
  76.6 0.0 copy-done.4
  76.6 1.3 fusion.9
  77.9 0.1 dot_general.20
  78.0 5.4 %fusion = f32[64,4,4096]{2,0,1:T(8,128)} fusion(bf16[1,512,4096]{2,1,0:T(8,128)(2,1)} %param.13, bf16[64,4,512]{2,1,0:T(4,128)(2,1)S(1)} %dot_general.20), kind=kOutput, calls=%fused_computation | convolution fusion | flops 1073741824 | bytes 8650752 | tf_op jit(solution)/shard_map/dot_general | solution.py:52
  83.3 0.0 copy-start.1
  83.3 0.0 copy-start.2
  83.3 0.0 copy-start.5
  83.3 0.0 copy-start.3
  83.3 0.0 reduce-scatter.2.cloned.1.call-update
  83.4 0.7 copy-done.1
  84.1 0.0 copy-done.2
  84.1 76.7 %psum.21 = f32[64]{0:T(128)S(1)} all-reduce(f32[64]{0:T(128)S(1)} %get-tuple-element.7), channel_id=1, replica_groups=mesh['group'=64,'rep'=4] {'group','rep'}, use_global_device_ids=true, to_apply=%region_1.0 | all-reduce | flops 64 | bytes 512 | tf_op jit(solution)/shard_map/psum | solution.py:24
  160.8 0.1 multiply_reduce_fusion.5
  160.9 0.1 multiply_reduce_fusion.4
  161.0 74.3 %psum.22 = f32[64]{0:T(128)S(1)} all-reduce(f32[64]{0:T(128)S(1)} %multiply_reduce_fusion.4), channel_id=1, replica_groups=mesh['group'=64,'rep'=4] {'group','rep'}, use_global_device_ids=true, to_apply=%region_4.0 | all-reduce | flops 64 | bytes 512 | tf_op jit(solution)/shard_map/psum | solution.py:24
  235.3 0.0 reduce-scatter.2.cloned.1.call-done
  235.3 1.3 convert_element_type.22
  236.6 1.2 copy.12
  237.8 8.1 %all-to-all-start.1 = ((bf16[64,4,1024]{2,1,0:T(4,128)(2,1)}), bf16[64,4,1024]{2,1,0:T(4,128)(2,1)S(1)}, u32[]{:S(2)}, u32[]{:S(2)}) async-start(bf16[64,4,1024]{2,1,0:T(4,128)(2,1)} %copy.12), calls=%async_computation.2 | async-start | bytes 1048576 | tf_op jit(solution)/shard_map/all_to_all | solution.py:58
  245.9 0.1 multiply_reduce_fusion.3
  246.0 0.0 copy-done.5
  246.0 0.6 dynamic-slice.1
  247.3 0.1 multiply_reduce_fusion.2
  247.4 76.3 %psum.23 = f32[64]{0:T(128)S(1)} all-reduce(f32[64]{0:T(128)S(1)} %multiply_reduce_fusion.2), channel_id=1, replica_groups=mesh['group'=64,'rep'=4] {'group','rep'}, use_global_device_ids=true, to_apply=%region_7.0 | all-reduce | flops 64 | bytes 512 | tf_op jit(solution)/shard_map/psum | solution.py:24
  323.7 0.0 copy-done.3
  323.7 0.1 dynamic-slice_bitcast_fusion
  323.8 0.2 multiply_reduce_fusion.1
  324.0 0.1 multiply_dynamic-update-slice_fusion
  324.1 7.7 %all-reduce = f32[128]{0:T(128)S(1)} all-reduce(f32[128]{0:T(128)S(1)} %multiply_dynamic-update-slice_fusion), channel_id=1, replica_groups=mesh['group'=64,'rep'=4] {'rep'}, use_global_device_ids=true, to_apply=%add | all-reduce | flops 128 | bytes 1024
  331.8 0.0 all-to-all-done.1
  331.8 0.1 reshape.33
  331.9 1.0 fusion.12
  (7 shorter events, 0.0 us)
Async XLA Ops:
  6.5 2.5 copy-start
  6.5 63.8 %all-gather.2.cloned.1.call-start = ((), (), s32[]{:S(2)}) async-start(), calls=%async_computation.3 | async-start | bytes 2621440 | tf_op jit(solution)/shard_map/all_gather | solution.py:41
  39.9 195.4 %reduce-scatter.2.cloned.1.call-start = ((), (), s32[]{:S(2)}) async-start(), calls=%async_computation.4 | async-start | bytes 5242880 | tf_op jit(solution)/shard_map/reduce_scatter | solution.py:55
  72.9 3.7 %copy-start.4 = (bf16[1,4096,512]{2,1,0:T(8,128)(2,1)S(1)}, bf16[1,4096,512]{2,1,0:T(8,128)(2,1)}, u32[]{:S(2)}) copy-start(bf16[1,4096,512]{2,1,0:T(8,128)(2,1)} %param.12) | copy-start | bytes 12582916
  83.3 0.7 copy-start.1
  83.3 0.7 copy-start.2
  83.3 162.7 %copy-start.5 = (u32[256]{0:T(256)S(1)}, u32[256]{0:T(256)}, u32[]{:S(2)}) copy-start(u32[256]{0:T(256)} %constant.38) | copy-start | bytes 3076
  83.3 240.3 %copy-start.3 = (s32[128,1]{0,1:T(1,128)S(1)}, s32[128,1]{0,1:T(1,128)}, u32[]{:S(2)}) copy-start(s32[128,1]{0,1:T(1,128)} %param.10) | copy-start | bytes 1540
  237.8 93.9 %all-to-all-start.1 = ((bf16[64,4,1024]{2,1,0:T(4,128)(2,1)}), bf16[64,4,1024]{2,1,0:T(4,128)(2,1)S(1)}, u32[]{:S(2)}, u32[]{:S(2)}) async-start(bf16[64,4,1024]{2,1,0:T(4,128)(2,1)} %copy.12), calls=%async_computation.2 | async-start | bytes 1048576 | tf_op jit(solution)/shard_map/all_to_all | solution.py:58
Sparse Core Ops, SparseCore 0:
  40.0 30.2 all-gather.1
  83.5 49.9 reduce-scatter.1
where the time goes:
time: 341 us; the launch traced here: 340 us
  blocking collectives  265 us (78%)
  waiting for transfers between devices  30.4 us (9%)
  between operations  14.2 us (4%)
  matrix products  11.6 us (3%)
  starting transfers between devices  8.11 us (2%)
  local copies, waits for them, and re-layouts  5.5 us (2%)
  other arithmetic  4.47 us (1%)
    psum x3, blocking collectives, local(): lax.psum(jnp.sum(kernel * row_scale[:, None], axis=0), ('group', 'rep'))  227 us
    all_gather x1, waiting for transfers between devices, local(): lax.all_gather(lax.all_to_all(outgoing, 'group', split_axis=0, concat_axi...  30.4 us
    all_to_all x1, blocking collectives, local(): lax.all_to_all(outgoing, 'group', split_axis=0, concat_axis=0, tiled=True)  30.4 us
    all_to_all x1, starting transfers between devices, local(): lax.all_to_all(summed, 'group', split_axis=0, concat_axis=0, tiled=True)  8.06 us
    unnamed x1, blocking collectives  7.72 us
  transfers between devices with their start and end apart: 3, of which 1 were waited for; matrix products, arithmetic and copies ran while one was open for 0% of the time, Pallas kernels for 0%

commit v1 on v0

v1 whole, which is shorter than its diff:
```python
import jax
import jax.numpy as jnp
from jax import lax
from jax.experimental import pallas as pl
from jax.experimental.pallas import tpu as pltpu
from jax.sharding import PartitionSpec as P

MESH = pl.DeviceIdType.MESH
PASSES = 3
NY, NZ, NC = 4, 8, 2
NX = 4
E = NY * NZ * NC
CAP = 4
TOK = 128
D = 4096
Q = D // NX
FH = 512
NB = NY
PB = NZ * NC
CW = 256
NCH = Q // CW
ROWS = PB * CAP
BR = ROWS * NCH
FW = 256
F32 = jnp.float32
BF16 = jnp.bfloat16


def iota(shape, dim):
    return lax.broadcasted_iota(jnp.int32, shape, dim)


def one_if(mask):
    return jnp.where(mask, 1.0, 0.0).astype(BF16)


def dot(a, b):
    return jnp.dot(a, b, preferred_element_type=F32)


def kernel_body(
    tokens, affinity, gumbel, assign, w_gate, w_up, w_down, out,
    wg, wu, wd, stack, outgoing, x_in, xs, hid, p_own, p_send, p_recv, ret, home, acc,
    kall, col_src, col_in,
    w_sem, k_send, k_recv, col_send, col_recv, d_send, d_recv, ag_send, ag_recv,
    rs_send, rs_recv, b_send, b_recv,
):
    g = lax.axis_index("group")
    r = lax.axis_index("rep")
    my_y = lax.div(g, NZ * NC)
    my_z = lax.rem(lax.div(g, NC), NZ)
    my_c = lax.rem(g, NC)

    def wrap(v, n):
        return jnp.where(v >= n, v - n, v)

    def ahead(i):
        y = wrap(my_y + lax.div(i, PB), NY)
        z = wrap(my_z + lax.rem(lax.div(i, NC), NZ), NZ)
        c = wrap(my_c + lax.rem(i, NC), NC)
        return (y * NZ + z) * NC + c

    def behind(i):
        y = wrap(my_y + NY - lax.div(i, PB), NY)
        z = wrap(my_z + NZ - lax.rem(lax.div(i, NC), NZ), NZ)
        c = wrap(my_c + NC - lax.rem(i, NC), NC)
        return (y * NZ + z) * NC + c

    def beside(d):
        return wrap(r + d, NX)

    def each(low, high, body):
        def step(i, carry):
            body(i)
            return carry

        lax.fori_loop(low, high, step, 0)

    def remote(src, dst, send, recv, device):
        return pltpu.make_async_remote_copy(
            src, dst, send, recv, device_id=device, device_id_type=MESH
        )

    def wait_bytes(ref, sem):
        pltpu.make_async_copy(ref, ref, sem).wait()

    barrier = pltpu.get_barrier_semaphore()
    for d in range(1, NX):
        pl.semaphore_signal(barrier, inc=1, device_id=(g, beside(d)), device_id_type=MESH)
    each(
        1,
        E,
        lambda i: pl.semaphore_signal(
            barrier, inc=1, device_id=(ahead(i), r), device_id_type=MESH
        ),
    )

    weights = [
        pltpu.make_async_copy(w_gate.at[0], wg, w_sem.at[0]),
        pltpu.make_async_copy(w_up.at[0], wu, w_sem.at[1]),
        pltpu.make_async_copy(w_down.at[0], wd, w_sem.at[2]),
    ]
    for copy in weights:
        copy.start()

    chosen = assign[...]
    onehot = (iota((E, TOK), 0) == chosen).astype(F32)
    before = one_if(iota((TOK, TOK), 0) < iota((TOK, TOK), 1))
    earlier = dot(onehot.astype(BF16), before)
    slot = jnp.sum(onehot * earlier, axis=0, keepdims=True).astype(jnp.int32)
    dy = lax.shift_right_logical(chosen, 4) - my_y
    dz = jnp.bitwise_and(lax.shift_right_logical(chosen, 1), NZ - 1) - my_z
    dc = jnp.bitwise_and(chosen, 1) - my_c
    dy = jnp.where(dy < 0, dy + NY, dy)
    dz = jnp.where(dz < 0, dz + NZ, dz)
    dc = jnp.where(dc < 0, dc + NC, dc)
    code = ((dy * NZ + dz) * NC + dc) * CAP + slot
    eye = iota((TOK, TOK), 0) == iota((TOK, TOK), 1)

    def as_column(v):
        v = jnp.broadcast_to(v.astype(F32), (TOK, TOK))
        return jnp.sum(jnp.where(eye, v, 0.0), axis=1, keepdims=True).astype(jnp.int32)

    code_col = as_column(code)
    chosen_col = as_column(chosen)

    for c in range(NCH):
        stack[c * TOK : (c + 1) * TOK, :] = tokens[:, c * CW : (c + 1) * CW]

    row = iota((BR, 1), 0)
    row_code = lax.shift_right_logical(row, 4) * CAP + jnp.bitwise_and(row, CAP - 1)
    row_chunk = jnp.bitwise_and(lax.shift_right_logical(row, 2), NCH - 1)
    lane = iota((1, BR), 1)
    lane_code = lax.shift_right_logical(lane, 4) * CAP + jnp.bitwise_and(lane, CAP - 1)
    lane_chunk = jnp.bitwise_and(lax.shift_right_logical(lane, 2), NCH - 1)

    for k in range(NB):
        placer = jnp.concatenate(
            [
                one_if(jnp.where(row_chunk == c, row_code + k * ROWS, -1) == code)
                for c in range(NCH)
            ],
            axis=1,
        )
        sent = dot(placer, stack[...]).astype(BF16)
        outgoing[k * PB : (k + 1) * PB] = sent.reshape(PB, NCH * CAP, CW)

    kall[pl.ds(r, 1)] = jnp.exp(affinity[...] + gumbel[...])[None]

    pl.semaphore_wait(barrier, E - 1 + NX - 1)

    k_copies = []
    for d in range(1, NX):
        copy = remote(
            kall.at[r], kall.at[r], k_send.at[d - 1], k_recv.at[d - 1], (g, beside(d))
        )
        copy.start()
        k_copies.append(copy)
    pltpu.make_async_copy(outgoing.at[0], x_in.at[0, r, 0], d_recv.at[0]).start()
    for k in range(NB):
        each(
            max(1, k * PB),
            (k + 1) * PB,
            lambda i, k=k: remote(
                outgoing.at[i], x_in.at[k, r, i - k * PB], d_send, d_recv.at[k], (ahead(i), r)
            ).start(),
        )

    def column_send(number, row_scale):
        scaled = kall[...] * row_scale
        col = jnp.sum(jnp.sum(scaled, axis=0), axis=0, keepdims=True)
        col = jnp.concatenate([col, jnp.zeros((1, 128 - E), F32)], axis=1)
        col_src[number] = col
        col_in[number, 0] = col
        each(
            1,
            E,
            lambda i: remote(
                col_src.at[number],
                col_in.at[number, i],
                col_send,
                col_recv.at[number],
                (ahead(i), r),
            ).start(),
        )

    def column_finish(number):
        wait_bytes(col_in.at[number, pl.ds(1, E - 1)], col_recv.at[number])
        total = jnp.sum(col_in[number], axis=0)
        col_scale = float(TOK) / total[:, :E]
        row_scale = 1.0 / jnp.sum(kall[...] * col_scale[None], axis=2, keepdims=True)
        return col_scale, row_scale

    def gather_send(k):
        wait_bytes(x_in.at[k, r], d_recv.at[k])
        for d in range(1, NX):
            remote(
                x_in.at[k, r], x_in.at[k, r], ag_send, ag_recv.at[k, d - 1], (g, beside(d))
            ).start()

    def gather_wait(k):
        for d in range(1, NX):
            wait_bytes(x_in.at[k, 0], ag_recv.at[k, d - 1])

    pick = one_if(
        iota((BR, BR), 1)
        == jnp.bitwise_and(lax.shift_right_logical(iota((BR, BR), 0), 2), PB - 1) * (NCH * CAP)
        + lax.shift_right_logical(iota((BR, BR), 0), 6) * CAP
        + jnp.bitwise_and(iota((BR, BR), 0), CAP - 1)
    )
    spread = one_if(
        iota((BR, BR), 0)
        == jnp.bitwise_and(lax.shift_right_logical(iota((BR, BR), 1), 2), PB - 1) * (NCH * CAP)
        + lax.shift_right_logical(iota((BR, BR), 1), 6) * CAP
        + jnp.bitwise_and(iota((BR, BR), 1), CAP - 1)
    )

    def experts(k):
        for q in range(NX):
            y = dot(pick, x_in[k, q].reshape(BR, CW)).astype(BF16)
            for c in range(NCH):
                at = q * Q + c * CW
                xs[:, at : at + CW] = y[c * ROWS : (c + 1) * ROWS]
        for n in range(FH // FW):
            cols = pl.ds(n * FW, FW)
            gate = dot(xs[...], wg[:, cols])
            up = dot(xs[...], wu[:, cols])
            hid[:, cols] = (gate / (1.0 + jnp.exp(-gate)) * up).astype(BF16)
        for d in (2, 1, 3, 0):
            at = beside(d) * Q if d else r * Q
            part = dot(hid[...], wd[:, pl.ds(pl.multiple_of(at, Q), Q)])
            if d:
                p_send[k, d - 1] = part.astype(BF16)
                remote(
                    p_send.at[k, d - 1],
                    p_recv.at[k, d - 1],
                    rs_send,
                    rs_recv.at[k, d - 1],
                    (g, beside(d)),
                ).start()
            else:
                p_own[k] = part

    def send_back(k):
        total = p_own[k]
        for d in range(1, NX):
            wait_bytes(p_recv.at[k, d - 1], rs_recv.at[k, d - 1])
            total = total + p_recv[k, d - 1].astype(F32)
        total = total.astype(BF16)
        chunks = jnp.concatenate(
            [total[:, c * CW : (c + 1) * CW] for c in range(NCH)], axis=0
        )
        sent = dot(spread, chunks).astype(BF16)
        ret[k * PB : (k + 1) * PB] = sent.reshape(PB, NCH * CAP, CW)
        if k == 0:
            pltpu.make_async_copy(ret.at[0], home.at[0], b_recv.at[0]).start()
        each(
            max(1, k * PB),
            (k + 1) * PB,
            lambda i: remote(
                ret.at[i], home.at[i], b_send, b_recv.at[k], (behind(i), r)
            ).start(),
        )

    def combine(k):
        rows = pl.ds(k * PB, PB)
        wait_bytes(home.at[rows], b_recv.at[k])
        landed = home[k * PB : (k + 1) * PB].reshape(BR, CW)
        for c in range(NCH):
            place = one_if(jnp.where(lane_chunk == c, lane_code + k * ROWS, -1) == code_col)
            part = dot(place, landed)
            if k == 0:
                acc[c] = part
            else:
                acc[c] += part

    for copy in k_copies:
        copy.wait_recv()
    column_send(0, jnp.ones((NX, TOK // NX, 1), F32))
    gather_send(0)
    gather_send(1)
    col_scale, row_scale = column_finish(0)
    column_send(1, row_scale)
    gather_send(2)
    gather_send(3)
    col_scale, row_scale = column_finish(1)
    column_send(2, row_scale)
    for copy in weights:
        copy.wait()
    gather_wait(0)
    experts(0)
    gather_wait(1)
    experts(1)
    send_back(0)
    gather_wait(2)
    experts(2)
    send_back(1)
    gather_wait(3)
    experts(3)
    send_back(2)
    col_scale, row_scale = column_finish(2)
    chosen_one = (iota((TOK, E), 1) == chosen_col).astype(F32).reshape(NX, TOK // NX, E)
    picked = jnp.sum(chosen_one * kall[...] * col_scale[None], axis=2, keepdims=True)
    weight = (float(E) * row_scale * picked).reshape(TOK, 1)
    combine(0)
    send_back(3)
    combine(1)
    combine(2)
    combine(3)
    for c in range(NCH):
        out[:, c * CW : (c + 1) * CW] = (weight * acc[c]).astype(BF16)

    for copy in k_copies:
        copy.wait_send()
    wait_bytes(outgoing.at[pl.ds(0, E - 1)], d_send)
    wait_bytes(col_in.at[pl.ds(0, PASSES), pl.ds(1, E - 1)], col_send)
    wait_bytes(x_in.at[pl.ds(0, NB), pl.ds(0, NX - 1)], ag_send)
    wait_bytes(p_send, rs_send)
    wait_bytes(ret.at[pl.ds(0, E - 1)], b_send)


def local(tokens, affinity, gumbel, assign, w_gate, w_up, w_down):
    dma = pltpu.SemaphoreType.DMA
    vmem = pl.BlockSpec(memory_space=pltpu.VMEM)
    hbm = pl.BlockSpec(memory_space=pl.ANY)
    return pl.pallas_call(
        kernel_body,
        out_shape=jax.ShapeDtypeStruct((TOK, Q), BF16),
        in_specs=[vmem, vmem, vmem, vmem, hbm, hbm, hbm],
        out_specs=vmem,
        scratch_shapes=[
            pltpu.VMEM((D, FH), BF16),
            pltpu.VMEM((D, FH), BF16),
            pltpu.VMEM((FH, D), BF16),
            pltpu.VMEM((NCH * TOK, CW), BF16),
            pltpu.VMEM((E, NCH * CAP, CW), BF16),
            pltpu.VMEM((NB, NX, PB, NCH * CAP, CW), BF16),
            pltpu.VMEM((ROWS, D), BF16),
            pltpu.VMEM((ROWS, FH), BF16),
            pltpu.VMEM((NB, ROWS, Q), F32),
            pltpu.VMEM((NB, NX - 1, ROWS, Q), BF16),
            pltpu.VMEM((NB, NX - 1, ROWS, Q), BF16),
            pltpu.VMEM((E, NCH * CAP, CW), BF16),
            pltpu.VMEM((E, NCH * CAP, CW), BF16),
            pltpu.VMEM((NCH, TOK, CW), F32),
            pltpu.VMEM((NX, TOK // NX, E), F32),
            pltpu.VMEM((PASSES, 1, 128), F32),
            pltpu.VMEM((PASSES, E, 1, 128), F32),
            dma((3,)),
            dma((NX - 1,)),
            dma((NX - 1,)),
            dma,
            dma((PASSES,)),
            dma,
            dma((NB,)),
            dma,
            dma((NB, NX - 1)),
            dma,
            dma((NB, NX - 1)),
            dma,
            dma((NB,)),
        ],
        compiler_params=pltpu.CompilerParams(
            collective_id=0, has_side_effects=True, vmem_limit_bytes=56 * 2**20
        ),
        cost_estimate=pl.CostEstimate(
            flops=3 * 2 * 256 * D * FH, bytes_accessed=13 * 2**20, transcendentals=2**17
        ),
        name="moe",
    )(tokens, affinity, gumbel, assign.reshape(1, TOK), w_gate, w_up, w_down)


def solution(mesh):
    return jax.shard_map(
        local,
        mesh=mesh,
        in_specs=(
            P("group", "rep"),
            P(("group", "rep"), None),
            P(("group", "rep"), None),
            P("group", None),
            P("group", None, "rep"),
            P("group", None, "rep"),
            P("group", "rep", None),
        ),
        out_specs=P("group", "rep"),
        check_vma=False,
    )
```

time: 341 us -> 78.2 us (0.23)
  blocking collectives: 265 us -> 0 us
  Pallas kernels: 0 us -> 76.4 us
  waiting for transfers between devices: 30.4 us -> 0 us
  between operations: 14.2 us -> 0.01 us
  matrix products: 11.6 us -> 0 us
  starting transfers between devices: 8.11 us -> 0 us
  other arithmetic: 4.47 us -> 0 us
  local copies, waits for them, and re-layouts: 5.5 us -> 1.67 us
    psum x3 -> x0, blocking collectives: 227 us -> none  [local(): lax.psum(jnp.sum(kernel * row_scale[:, None], axis=0), ('group', 'rep'))]
    pallas_call x0 -> x1, Pallas kernels: none -> 76.4 us  [local(): pl.pallas_call(kernel_body, out_shape=jax.ShapeDtypeStruct((TOK, Q), BF16...]
    all_gather x1 -> x0, waiting for transfers between devices: 30.4 us -> none  [local(): lax.all_gather(lax.all_to_all(outgoing, 'group', split_axis=0, concat_axi...]
    all_to_all x1 -> x0, blocking collectives: 30.4 us -> none  [local(): lax.all_to_all(outgoing, 'group', split_axis=0, concat_axis=0, tiled=True)]
    dot_general x5 -> x0, matrix products: 11.6 us -> none  [the longest x1 5.38 us: local(): jnp.dot(hidden, expert_down[0], preferred_element_type=jnp.float32)]
    all_to_all x1 -> x0, starting transfers between devices: 8.06 us -> none  [local(): lax.all_to_all(summed, 'group', split_axis=0, concat_axis=0, tiled=True)]
    unnamed x1 -> x0, blocking collectives: 7.72 us -> none
  transfers between devices with their start and end apart: 3 -> 0, of which waited for: 1 -> 0; matrix products, arithmetic and copies ran while one was open for 0% -> 0% of each run, Pallas kernels for 0% -> 0%
where the time goes in v1:
time: 78.2 us; the launch traced here: 78 us
  Pallas kernels  76.4 us (98%)
  local copies, waits for them, and re-layouts  1.67 us (2%)
    pallas_call x1, Pallas kernels, local(): pl.pallas_call(kernel_body, out_shape=jax.ShapeDtypeStruct((TOK, Q), BF16...  76.4 us
    unnamed x1, local copies, waits for them, and re-layouts  1.67 us

profile of v1, /device:TPU:1, one launch (start us, length us, event | category | flops | bytes accessed | tf_op | source)
XLA Modules:
  0.0 78.0 jit_solution(6939333554889918789)
XLA Ops:
  0.0 76.4 %moe.1 = bf16[128,1024]{1,0:T(8,128)(2,1)} custom-call(bf16[128,1024]{1,0:T(8,128)(2,1)} %tokens.1, f32[32,64]{1,0:T(8,128)} %affinity.1, f32[32,64]{1,0:T(8,128)} %gumbel.1, s32[1,128]{1,0:T(1,128)} %bitcast.1, bf16[1,4096,512]{2,1,0:T(8,128)(2,1)} %w_gate.1, bf16[1,4096,512]{2,1,0:T(8,128)(2,1)} %w_up.1, bf16[1,512,4096]{2,1,0:T(8,128)(2,1)} %w_down.1), custom_call_target="tpu_custom_call" | custom-call | flops 3221225472 | bytes 13631488 | tf_op jit(solution)/shard_map/moe/pallas_call | solution.py:326
  76.4 1.7 %copy.9 = bf16[128,1024]{1,0:T(8,128)(2,1)} copy(bf16[128,1024]{1,0:T(8,128)(2,1)} %moe.1) | data formatting | bytes 524288

commit v2 on v1

--- a/solution.py
+++ b/solution.py
@@ -20,6 +20,7 @@
 CW = 256
 NCH = Q // CW
 ROWS = PB * CAP
+HR = ROWS // 2
 BR = ROWS * NCH
 FW = 256
 F32 = jnp.float32
@@ -40,7 +41,7 @@
 
 def kernel_body(
     tokens, affinity, gumbel, assign, w_gate, w_up, w_down, out,
-    wg, wu, wd, stack, outgoing, x_in, xs, hid, p_own, p_send, p_recv, ret, home, acc,
+    wg, wu, wd, stack, outgoing, x_in, xs, hid, p_own, p_late, p_send, p_relay, p_recv, ret, home, acc,
     kall, col_src, col_in,
     w_sem, k_send, k_recv, col_send, col_recv, d_send, d_recv, ag_send, ag_recv,
     rs_send, rs_recv, b_send, b_recv,
@@ -193,14 +194,21 @@
 
     def gather_send(k):
         wait_bytes(x_in.at[k, r], d_recv.at[k])
-        for d in range(1, NX):
+        for way, d in enumerate((1, NX - 1)):
             remote(
-                x_in.at[k, r], x_in.at[k, r], ag_send, ag_recv.at[k, d - 1], (g, beside(d))
+                x_in.at[k, r], x_in.at[k, r], ag_send, ag_recv.at[k, way], (g, beside(d))
             ).start()
 
+    def gather_pass_on(k):
+        for way, d in enumerate((1, NX - 1)):
+            source = beside(NX - d)
+            wait_bytes(x_in.at[k, 0], ag_recv.at[k, way])
+            half = x_in.at[k, source, pl.ds(way * (PB // 2), PB // 2)]
+            remote(half, half, ag_send, ag_recv.at[k, 2 + way], (g, beside(d))).start()
+
     def gather_wait(k):
-        for d in range(1, NX):
-            wait_bytes(x_in.at[k, 0], ag_recv.at[k, d - 1])
+        for way in range(2):
+            wait_bytes(x_in.at[k, 0, pl.ds(0, PB // 2)], ag_recv.at[k, 2 + way])
 
     pick = one_if(
         iota((BR, BR), 1)
@@ -229,23 +237,50 @@
         for d in (2, 1, 3, 0):
             at = beside(d) * Q if d else r * Q
             part = dot(hid[...], wd[:, pl.ds(pl.multiple_of(at, Q), Q)])
-            if d:
-                p_send[k, d - 1] = part.astype(BF16)
+            if d == 0:
+                p_own[k] = part
+            elif d == 2:
+                p_send[k, 1] = part.astype(BF16)
+                for way in range(2):
+                    remote(
+                        p_send.at[k, 1, pl.ds(way * HR, HR)],
+                        p_relay.at[k, way],
+                        rs_send,
+                        rs_recv.at[k, way],
+                        (g, beside(1 if way == 0 else NX - 1)),
+                    ).start()
+            else:
+                way = 0 if d == 1 else 1
+                now = pl.ds((1 - way) * HR, HR)
+                p_late[k, way] = part[way * HR : (way + 1) * HR]
+                p_send[k, d - 1, now] = part[(1 - way) * HR : (2 - way) * HR].astype(BF16)
                 remote(
-                    p_send.at[k, d - 1],
-                    p_recv.at[k, d - 1],
+                    p_send.at[k, d - 1, now],
+                    p_recv.at[k, way, now],
                     rs_send,
-                    rs_recv.at[k, d - 1],
+                    rs_recv.at[k, 2 + way],
                     (g, beside(d)),
                 ).start()
-            else:
-                p_own[k] = part
+
+    def relay(k):
+        for way in range(2):
+            d = 1 if way == 0 else NX - 1
+            late = pl.ds(way * HR, HR)
+            wait_bytes(p_relay.at[k, way], rs_recv.at[k, way])
+            p_send[k, d - 1, late] = (p_late[k, way] + p_relay[k, way].astype(F32)).astype(BF16)
+            remote(
+                p_send.at[k, d - 1, late],
+                p_recv.at[k, way, late],
+                rs_send,
+                rs_recv.at[k, 2 + way],
+                (g, beside(d)),
+            ).start()
 
     def send_back(k):
         total = p_own[k]
-        for d in range(1, NX):
-            wait_bytes(p_recv.at[k, d - 1], rs_recv.at[k, d - 1])
-            total = total + p_recv[k, d - 1].astype(F32)
+        for way in range(2):
+            wait_bytes(p_recv.at[k, way], rs_recv.at[k, 2 + way])
+            total = total + p_recv[k, way].astype(F32)
         total = total.astype(BF16)
         chunks = jnp.concatenate(
             [total[:, c * CW : (c + 1) * CW] for c in range(NCH)], axis=0
@@ -279,24 +314,32 @@
     column_send(0, jnp.ones((NX, TOK // NX, 1), F32))
     gather_send(0)
     gather_send(1)
+    gather_pass_on(0)
+    gather_send(2)
+    gather_pass_on(1)
+    gather_send(3)
+    gather_pass_on(2)
     col_scale, row_scale = column_finish(0)
     column_send(1, row_scale)
-    gather_send(2)
-    gather_send(3)
-    col_scale, row_scale = column_finish(1)
-    column_send(2, row_scale)
     for copy in weights:
         copy.wait()
     gather_wait(0)
     experts(0)
+    gather_pass_on(3)
     gather_wait(1)
     experts(1)
-    send_back(0)
+    relay(0)
     gather_wait(2)
     experts(2)
-    send_back(1)
+    relay(1)
+    col_scale, row_scale = column_finish(1)
+    column_send(2, row_scale)
+    send_back(0)
     gather_wait(3)
     experts(3)
+    relay(2)
+    send_back(1)
+    relay(3)
     send_back(2)
     col_scale, row_scale = column_finish(2)
     chosen_one = (iota((TOK, E), 1) == chosen_col).astype(F32).reshape(NX, TOK // NX, E)
@@ -338,8 +381,10 @@
             pltpu.VMEM((ROWS, D), BF16),
             pltpu.VMEM((ROWS, FH), BF16),
             pltpu.VMEM((NB, ROWS, Q), F32),
+            pltpu.VMEM((NB, 2, HR, Q), F32),
             pltpu.VMEM((NB, NX - 1, ROWS, Q), BF16),
-            pltpu.VMEM((NB, NX - 1, ROWS, Q), BF16),
+            pltpu.VMEM((NB, 2, HR, Q), BF16),
+            pltpu.VMEM((NB, 2, ROWS, Q), BF16),
             pltpu.VMEM((E, NCH * CAP, CW), BF16),
             pltpu.VMEM((E, NCH * CAP, CW), BF16),
             pltpu.VMEM((NCH, TOK, CW), F32),
@@ -354,9 +399,9 @@
             dma,
             dma((NB,)),
             dma,
-            dma((NB, NX - 1)),
+            dma((NB, 4)),
             dma,
-            dma((NB, NX - 1)),
+            dma((NB, 4)),
             dma,
             dma((NB,)),
         ],

time: 78.2 us -> 67.6 us (0.86)
  Pallas kernels: 76.4 us -> 65.8 us
    pallas_call x1, Pallas kernels: 76.4 us -> 65.8 us  [local(): pl.pallas_call(kernel_body, out_shape=jax.ShapeDtypeStruct((TOK, Q), BF16...]
where the time goes in v2:
time: 67.6 us; the launch traced here: 67.4 us
  Pallas kernels  65.8 us (97%)
  local copies, waits for them, and re-layouts  1.67 us (2%)
    pallas_call x1, Pallas kernels, local(): pl.pallas_call(kernel_body, out_shape=jax.ShapeDtypeStruct((TOK, Q), BF16...  65.8 us
    unnamed x1, local copies, waits for them, and re-layouts  1.67 us

profile of v2, /device:TPU:1, one launch (start us, length us, event | category | flops | bytes accessed | tf_op | source)
XLA Modules:
  0.0 67.4 jit_solution(2358411877978114311)
XLA Ops:
  0.0 65.8 %moe.1 = bf16[128,1024]{1,0:T(8,128)(2,1)} custom-call(bf16[128,1024]{1,0:T(8,128)(2,1)} %tokens.1, f32[32,64]{1,0:T(8,128)} %affinity.1, f32[32,64]{1,0:T(8,128)} %gumbel.1, s32[1,128]{1,0:T(1,128)} %bitcast.1, bf16[1,4096,512]{2,1,0:T(8,128)(2,1)} %w_gate.1, bf16[1,4096,512]{2,1,0:T(8,128)(2,1)} %w_up.1, bf16[1,512,4096]{2,1,0:T(8,128)(2,1)} %w_down.1), custom_call_target="tpu_custom_call" | custom-call | flops 3221225472 | bytes 13631488 | tf_op jit(solution)/shard_map/moe/pallas_call | solution.py:369
  65.8 1.7 %copy.9 = bf16[128,1024]{1,0:T(8,128)(2,1)} copy(bf16[128,1024]{1,0:T(8,128)(2,1)} %moe.1) | data formatting | bytes 524288

commit v3 on v2

--- a/solution.py
+++ b/solution.py
@@ -42,8 +42,8 @@
 def kernel_body(
     tokens, affinity, gumbel, assign, w_gate, w_up, w_down, out,
     wg, wu, wd, stack, outgoing, x_in, xs, hid, p_own, p_late, p_send, p_relay, p_recv, ret, home, acc,
-    kall, col_src, col_in,
-    w_sem, k_send, k_recv, col_send, col_recv, d_send, d_recv, ag_send, ag_recv,
+    kall, col_src, col_in, place,
+    plane_sem, w_sem, k_send, k_recv, col_send, col_recv, d_send, d_recv, ag_send, ag_recv,
     rs_send, rs_recv, b_send, b_recv,
 ):
     g = lax.axis_index("group")
@@ -55,27 +55,22 @@
     def wrap(v, n):
         return jnp.where(v >= n, v - n, v)
 
+    at_y = [wrap(my_y + d, NY) * PB for d in range(NY)]
+    at_z = [wrap(my_z + d, NZ) * NC for d in range(NZ)]
+    at_c = [wrap(my_c + d, NC) for d in range(NC)]
+
     def ahead(i):
-        y = wrap(my_y + lax.div(i, PB), NY)
-        z = wrap(my_z + lax.rem(lax.div(i, NC), NZ), NZ)
-        c = wrap(my_c + lax.rem(i, NC), NC)
-        return (y * NZ + z) * NC + c
+        return at_y[i // PB] + at_z[i // NC % NZ] + at_c[i % NC]
 
     def behind(i):
-        y = wrap(my_y + NY - lax.div(i, PB), NY)
-        z = wrap(my_z + NZ - lax.rem(lax.div(i, NC), NZ), NZ)
-        c = wrap(my_c + NC - lax.rem(i, NC), NC)
-        return (y * NZ + z) * NC + c
+        return at_y[-(i // PB) % NY] + at_z[-(i // NC) % NZ] + at_c[-i % NC]
 
     def beside(d):
         return wrap(r + d, NX)
 
     def each(low, high, body):
-        def step(i, carry):
+        for i in range(low, high):
             body(i)
-            return carry
-
-        lax.fori_loop(low, high, step, 0)
 
     def remote(src, dst, send, recv, device):
         return pltpu.make_async_remote_copy(
@@ -90,11 +85,13 @@
         pl.semaphore_signal(barrier, inc=1, device_id=(g, beside(d)), device_id_type=MESH)
     each(
         1,
-        E,
+        PB,
         lambda i: pl.semaphore_signal(
             barrier, inc=1, device_id=(ahead(i), r), device_id_type=MESH
         ),
     )
+    for d in range(1, NY):
+        pl.semaphore_signal(barrier, inc=1, device_id=(ahead(d * PB), r), device_id_type=MESH)
 
     weights = [
         pltpu.make_async_copy(w_gate.at[0], wg, w_sem.at[0]),
@@ -148,7 +145,9 @@
 
     kall[pl.ds(r, 1)] = jnp.exp(affinity[...] + gumbel[...])[None]
 
-    pl.semaphore_wait(barrier, E - 1 + NX - 1)
+    pl.semaphore_wait(barrier, PB - 1 + NY - 1 + NX - 1)
+    for d in range(1, NY):
+        pl.semaphore_signal(plane_sem, inc=1, device_id=(ahead(d * PB), r), device_id_type=MESH)
 
     k_copies = []
     for d in range(1, NX):
@@ -158,14 +157,19 @@
         copy.start()
         k_copies.append(copy)
     pltpu.make_async_copy(outgoing.at[0], x_in.at[0, r, 0], d_recv.at[0]).start()
-    for k in range(NB):
+
+    def dispatch(k):
         each(
             max(1, k * PB),
             (k + 1) * PB,
-            lambda i, k=k: remote(
+            lambda i: remote(
                 outgoing.at[i], x_in.at[k, r, i - k * PB], d_send, d_recv.at[k], (ahead(i), r)
             ).start(),
         )
+
+    dispatch(0)
+    pl.semaphore_wait(plane_sem, NY - 1)
+    dispatch(1)
 
     def column_send(number, row_scale):
         scaled = kall[...] * row_scale
@@ -297,30 +301,38 @@
             ).start(),
         )
 
+    def make_place(k):
+        for c in range(NCH):
+            place[k, c * TOK : (c + 1) * TOK] = one_if(
+                jnp.where(lane_chunk == c, lane_code + k * ROWS, -1) == code_col
+            )
+
     def combine(k):
         rows = pl.ds(k * PB, PB)
         wait_bytes(home.at[rows], b_recv.at[k])
         landed = home[k * PB : (k + 1) * PB].reshape(BR, CW)
-        for c in range(NCH):
-            place = one_if(jnp.where(lane_chunk == c, lane_code + k * ROWS, -1) == code_col)
-            part = dot(place, landed)
-            if k == 0:
-                acc[c] = part
-            else:
-                acc[c] += part
+        part = dot(place[k], landed)
+        if k == 0:
+            acc[...] = part
+        else:
+            acc[...] += part
 
     for copy in k_copies:
         copy.wait_recv()
     column_send(0, jnp.ones((NX, TOK // NX, 1), F32))
+    for k in range(NB):
+        make_place(k)
     gather_send(0)
+    dispatch(2)
     gather_send(1)
+    dispatch(3)
     gather_pass_on(0)
     gather_send(2)
     gather_pass_on(1)
     gather_send(3)
-    gather_pass_on(2)
     col_scale, row_scale = column_finish(0)
     column_send(1, row_scale)
+    gather_pass_on(2)
     for copy in weights:
         copy.wait()
     gather_wait(0)
@@ -329,29 +341,27 @@
     gather_wait(1)
     experts(1)
     relay(0)
+    col_scale, row_scale = column_finish(1)
+    column_send(2, row_scale)
     gather_wait(2)
     experts(2)
     relay(1)
-    col_scale, row_scale = column_finish(1)
-    column_send(2, row_scale)
     send_back(0)
+    col_scale, row_scale = column_finish(2)
+    chosen_one = (iota((TOK, E), 1) == chosen_col).astype(F32).reshape(NX, TOK // NX, E)
+    picked = jnp.sum(chosen_one * kall[...] * col_scale[None], axis=2, keepdims=True)
+    weight = (float(E) * row_scale * picked).reshape(TOK, 1)
     gather_wait(3)
     experts(3)
     relay(2)
     send_back(1)
     relay(3)
     send_back(2)
-    col_scale, row_scale = column_finish(2)
-    chosen_one = (iota((TOK, E), 1) == chosen_col).astype(F32).reshape(NX, TOK // NX, E)
-    picked = jnp.sum(chosen_one * kall[...] * col_scale[None], axis=2, keepdims=True)
-    weight = (float(E) * row_scale * picked).reshape(TOK, 1)
-    combine(0)
     send_back(3)
-    combine(1)
-    combine(2)
-    combine(3)
+    for k in range(NB):
+        combine(k)
     for c in range(NCH):
-        out[:, c * CW : (c + 1) * CW] = (weight * acc[c]).astype(BF16)
+        out[:, c * CW : (c + 1) * CW] = (weight * acc[c * TOK : (c + 1) * TOK]).astype(BF16)
 
     for copy in k_copies:
         copy.wait_send()
@@ -387,10 +397,12 @@
             pltpu.VMEM((NB, 2, ROWS, Q), BF16),
             pltpu.VMEM((E, NCH * CAP, CW), BF16),
             pltpu.VMEM((E, NCH * CAP, CW), BF16),
-            pltpu.VMEM((NCH, TOK, CW), F32),
+            pltpu.VMEM((NCH * TOK, CW), F32),
             pltpu.VMEM((NX, TOK // NX, E), F32),
             pltpu.VMEM((PASSES, 1, 128), F32),
             pltpu.VMEM((PASSES, E, 1, 128), F32),
+            pltpu.VMEM((NB, NCH * TOK, BR), BF16),
+            pltpu.SemaphoreType.REGULAR,
             dma((3,)),
             dma((NX - 1,)),
             dma((NX - 1,)),

time: 67.6 us -> 65.7 us (0.972)
  Pallas kernels: 65.8 us -> 63.9 us
    pallas_call x1, Pallas kernels: 65.8 us -> 63.9 us  [local(): pl.pallas_call(kernel_body, out_shape=jax.ShapeDtypeStruct((TOK, Q), BF16...]
where the time goes in v3:
time: 65.7 us; the launch traced here: 65.6 us
  Pallas kernels  63.9 us (97%)
  local copies, waits for them, and re-layouts  1.67 us (3%)
    pallas_call x1, Pallas kernels, local(): pl.pallas_call(kernel_body, out_shape=jax.ShapeDtypeStruct((TOK, Q), BF16...  63.9 us
    unnamed x1, local copies, waits for them, and re-layouts  1.67 us

profile of v3, /device:TPU:1, one launch (start us, length us, event | category | flops | bytes accessed | tf_op | source)
XLA Modules:
  0.0 65.6 jit_solution(14908780297484614189)
XLA Ops:
  0.0 63.9 %moe.1 = bf16[128,1024]{1,0:T(8,128)(2,1)} custom-call(bf16[128,1024]{1,0:T(8,128)(2,1)} %tokens.1, f32[32,64]{1,0:T(8,128)} %affinity.1, f32[32,64]{1,0:T(8,128)} %gumbel.1, s32[1,128]{1,0:T(1,128)} %bitcast.1, bf16[1,4096,512]{2,1,0:T(8,128)(2,1)} %w_gate.1, bf16[1,4096,512]{2,1,0:T(8,128)(2,1)} %w_up.1, bf16[1,512,4096]{2,1,0:T(8,128)(2,1)} %w_down.1), custom_call_target="tpu_custom_call" | custom-call | flops 3221225472 | bytes 13631488 | tf_op jit(solution)/shard_map/moe/pallas_call | solution.py:379
  63.9 1.7 %copy.9 = bf16[128,1024]{1,0:T(8,128)(2,1)} copy(bf16[128,1024]{1,0:T(8,128)(2,1)} %moe.1) | data formatting | bytes 524288

commit v4 on v3

--- a/solution.py
+++ b/solution.py
@@ -69,7 +69,7 @@
         return wrap(r + d, NX)
 
     def each(low, high, body):
-        for i in range(low, high):
+        for i in sorted(range(low, high), key=lambda i: (-min(i // NC % NZ, NZ - i // NC % NZ), i)):
             body(i)
 
     def remote(src, dst, send, recv, device):
@@ -330,27 +330,23 @@
     gather_send(2)
     gather_pass_on(1)
     gather_send(3)
-    col_scale, row_scale = column_finish(0)
-    column_send(1, row_scale)
-    gather_pass_on(2)
     for copy in weights:
         copy.wait()
     gather_wait(0)
     experts(0)
+    gather_pass_on(2)
     gather_pass_on(3)
+    col_scale, row_scale = column_finish(0)
+    column_send(1, row_scale)
     gather_wait(1)
     experts(1)
     relay(0)
-    col_scale, row_scale = column_finish(1)
-    column_send(2, row_scale)
     gather_wait(2)
     experts(2)
     relay(1)
+    col_scale, row_scale = column_finish(1)
+    column_send(2, row_scale)
     send_back(0)
-    col_scale, row_scale = column_finish(2)
-    chosen_one = (iota((TOK, E), 1) == chosen_col).astype(F32).reshape(NX, TOK // NX, E)
-    picked = jnp.sum(chosen_one * kall[...] * col_scale[None], axis=2, keepdims=True)
-    weight = (float(E) * row_scale * picked).reshape(TOK, 1)
     gather_wait(3)
     experts(3)
     relay(2)
@@ -358,6 +354,10 @@
     relay(3)
     send_back(2)
     send_back(3)
+    col_scale, row_scale = column_finish(2)
+    chosen_one = (iota((TOK, E), 1) == chosen_col).astype(F32).reshape(NX, TOK // NX, E)
+    picked = jnp.sum(chosen_one * kall[...] * col_scale[None], axis=2, keepdims=True)
+    weight = (float(E) * row_scale * picked).reshape(TOK, 1)
     for k in range(NB):
         combine(k)
     for c in range(NCH):

time: 65.7 us -> 64.6 us (0.983)
  Pallas kernels: 63.9 us -> 62.8 us
    pallas_call x1, Pallas kernels: 63.9 us -> 62.8 us  [local(): pl.pallas_call(kernel_body, out_shape=jax.ShapeDtypeStruct((TOK, Q), BF16...]
where the time goes in v4:
time: 64.6 us; the launch traced here: 64.5 us
  Pallas kernels  62.8 us (97%)
  local copies, waits for them, and re-layouts  1.67 us (3%)
    pallas_call x1, Pallas kernels, local(): pl.pallas_call(kernel_body, out_shape=jax.ShapeDtypeStruct((TOK, Q), BF16...  62.8 us
    unnamed x1, local copies, waits for them, and re-layouts  1.67 us

profile of v4, /device:TPU:1, one launch (start us, length us, event | category | flops | bytes accessed | tf_op | source)
XLA Modules:
  0.0 64.5 jit_solution(458806231492680935)
XLA Ops:
  0.0 62.8 %moe.1 = bf16[128,1024]{1,0:T(8,128)(2,1)} custom-call(bf16[128,1024]{1,0:T(8,128)(2,1)} %tokens.1, f32[32,64]{1,0:T(8,128)} %affinity.1, f32[32,64]{1,0:T(8,128)} %gumbel.1, s32[1,128]{1,0:T(1,128)} %bitcast.1, bf16[1,4096,512]{2,1,0:T(8,128)(2,1)} %w_gate.1, bf16[1,4096,512]{2,1,0:T(8,128)(2,1)} %w_up.1, bf16[1,512,4096]{2,1,0:T(8,128)(2,1)} %w_down.1), custom_call_target="tpu_custom_call" | custom-call | flops 3221225472 | bytes 13631488 | tf_op jit(solution)/shard_map/moe/pallas_call | solution.py:379
  62.8 1.7 %copy.9 = bf16[128,1024]{1,0:T(8,128)(2,1)} copy(bf16[128,1024]{1,0:T(8,128)(2,1)} %moe.1) | data formatting | bytes 524288

commit v5 on v4

--- a/solution.py
+++ b/solution.py
@@ -350,8 +350,8 @@
     gather_wait(3)
     experts(3)
     relay(2)
+    relay(3)
     send_back(1)
-    relay(3)
     send_back(2)
     send_back(3)
     col_scale, row_scale = column_finish(2)

time: 64.6 us -> 66 us (1.022)
  Pallas kernels: 62.8 us -> 64.2 us
    pallas_call x1, Pallas kernels: 62.8 us -> 64.2 us  [local(): pl.pallas_call(kernel_body, out_shape=jax.ShapeDtypeStruct((TOK, Q), BF16...]
where the time goes in v5:
time: 66 us; the launch traced here: 65.9 us
  Pallas kernels  64.2 us (97%)
  local copies, waits for them, and re-layouts  1.67 us (3%)
    pallas_call x1, Pallas kernels, local(): pl.pallas_call(kernel_body, out_shape=jax.ShapeDtypeStruct((TOK, Q), BF16...  64.2 us
    unnamed x1, local copies, waits for them, and re-layouts  1.67 us

profile of v5, /device:TPU:1, one launch (start us, length us, event | category | flops | bytes accessed | tf_op | source)
XLA Modules:
  0.0 65.9 jit_solution(6963538300555475272)
XLA Ops:
  0.0 64.2 %moe.1 = bf16[128,1024]{1,0:T(8,128)(2,1)} custom-call(bf16[128,1024]{1,0:T(8,128)(2,1)} %tokens.1, f32[32,64]{1,0:T(8,128)} %affinity.1, f32[32,64]{1,0:T(8,128)} %gumbel.1, s32[1,128]{1,0:T(1,128)} %bitcast.1, bf16[1,4096,512]{2,1,0:T(8,128)(2,1)} %w_gate.1, bf16[1,4096,512]{2,1,0:T(8,128)(2,1)} %w_up.1, bf16[1,512,4096]{2,1,0:T(8,128)(2,1)} %w_down.1), custom_call_target="tpu_custom_call" | custom-call | flops 3221225472 | bytes 13631488 | tf_op jit(solution)/shard_map/moe/pallas_call | solution.py:379
  64.2 1.7 %copy.9 = bf16[128,1024]{1,0:T(8,128)(2,1)} copy(bf16[128,1024]{1,0:T(8,128)(2,1)} %moe.1) | data formatting | bytes 524288
